TPU v7x, 128 devices: a whole 4x4x4 slice. The times are simulated.
128 devices in a mesh: layer: 16 (over z, x), tok: 8 (over y, core).
Axes of the slice: x: 4, y: 4, z: 4, core: 2. Of those that a mesh axis runs over, the one named last changes fastest.
Arguments:
- activations: bfloat16 [16, 8192, 4096], P('layer', 'tok'), may hold values from -40 to 40, as said below
- sketch: bfloat16 [16, 4096, 512], P('layer'), may hold values from -0.0234375 to 0.0234375
Outputs:
- range_basis: float32 [8, 16, 64, 512], P('tok', 'layer')
- triangle: float32 [512, 512], replicated
- decoder: float32 [512, 16, 4096], P(None, 'layer', 'tok')
Inputs may be any that keep to these rules, and one draw needn't show every extreme that they name: `activations`: activations of order one to several, with magnitudes that vary from token to token.
All inputs are finite; a program needn't handle non-finite values.
Results may differ from a plain program's by a relative error of at most 0.0028.
Values may be sent and summed in bfloat16 or wider, within the bound.
A program may use at most 128 MiB of HBM per device.

v0:
```python
import math

import jax
import jax.numpy as jnp
from jax import lax
from jax.sharding import PartitionSpec as P


def swapped(value, axis, bit):
    mask = 2**bit
    pairs = [(source, source ^ mask) for source in range(lax.axis_size(axis))]
    return lax.ppermute(value, axis, pairs)


def on_device(activations, sketch):
    layer_rows = activations.shape[1]
    rank_cols = sketch.shape[2]
    layer_count = lax.axis_size("layer")
    tok_count = lax.axis_size("tok")
    total_rows = layer_rows * tok_count
    own_rows = layer_rows // layer_count
    block_rows = activations[0]
    summed = jnp.dot(block_rows, sketch[0], preferred_element_type=jnp.float32)
    sample = lax.psum_scatter(summed, "layer", scatter_dimension=0, tiled=True)
    own_gram = jnp.dot(
        sample.T, sample, precision=lax.Precision.HIGHEST, preferred_element_type=jnp.float32
    )
    gram_matrix = own_gram
    for bit_index in range(layer_count.bit_length() - 1):
        gram_matrix = gram_matrix + swapped(gram_matrix, "layer", bit_index)
    for bit_index in range(tok_count.bit_length() - 1):
        gram_matrix = gram_matrix + swapped(gram_matrix, "tok", bit_index)
    gram_matrix = gram_matrix / total_rows
    cholesky_factor = jnp.linalg.cholesky(gram_matrix)
    triangle = cholesky_factor.T
    basis_local = jax.scipy.linalg.solve_triangular(cholesky_factor, sample.T, lower=True).T
    range_basis = basis_local.reshape(1, 1, own_rows, rank_cols)
    narrow = basis_local.astype(jnp.bfloat16)
    normaliser = 1.0 / math.sqrt(total_rows)
    partial_value = jnp.einsum(
        "nr,lnd->rld",
        lax.all_gather(narrow, "layer", axis=0, tiled=True),
        activations,
        preferred_element_type=jnp.float32,
    )
    summed = lax.psum_scatter(partial_value, "tok", scatter_dimension=2, tiled=True)
    decoder = summed * normaliser
    return (range_basis, triangle, decoder)


def solution(mesh):
    return jax.shard_map(
        on_device,
        mesh=mesh,
        in_specs=(P("layer", "tok", None), P("layer", None, None)),
        out_specs=(P("tok", "layer", None, None), P(), P(None, "layer", "tok")),
        check_vma=False,
    )
```

profile of v0, /device:TPU:1, one launch (start us, length us, event | category | flops | bytes accessed | tf_op | source)
XLA Modules:
  0.0 494.2 jit_solution(14988995154635568616)
XLA Ops:
  7.2 10.4 %fusion.2 = f32[1024,512]{1,0:T(8,128)} fusion(bf16[1,1024,4096]{2,1,0:T(8,128)(2,1)} %param.2, bf16[1,4096,512]{2,1,0:T(8,128)(2,1)} %param.3), kind=kOutput, calls=%fused_computation.4 | convolution fusion | flops 4294967296 | bytes 14680064 | tf_op jit(solution)/shard_map/dot_general | solution.py:23
  17.7 76.1 %reduce-scatter.3.cloned.1.call-done = f32[64,512]{1,0:T(8,128)} async-done(((f32[1024,512]{1,0:T(8,128)}), f32[64,512]{1,0:T(8,128)}) %reduce-scatter.3.cloned.1.call-update) | async-done | bytes 131088 | tf_op jit(solution)/shard_map/reduce_scatter | solution.py:24
  93.8 2.0 fusion.42
  96.4 21.9 %collective-permute-done = f32[512,512]{0,1:T(8,128)S(1)} collective-permute-done((f32[512,512]{0,1:T(8,128)S(1)}, f32[512,512]{0,1:T(8,128)S(1)}, u32[]{:S(2)}, u32[]{:S(2)}) %collective-permute-start) | collective-permute-done | bytes 1048608 | tf_op jit(solution)/shard_map/ppermute | solution.py:12
  119.7 21.8 %collective-permute-done.1 = f32[512,512]{0,1:T(8,128)S(1)} collective-permute-done((f32[512,512]{0,1:T(8,128)S(1)}, f32[512,512]{0,1:T(8,128)S(1)}, u32[]{:S(2)}, u32[]{:S(2)}) %collective-permute-start.1) | collective-permute-done | bytes 1048608 | tf_op jit(solution)/shard_map/ppermute | solution.py:12
  141.8 20.5 %collective-permute-done.2 = f32[512,512]{0,1:T(8,128)S(1)} collective-permute-done((f32[512,512]{0,1:T(8,128)S(1)}, f32[512,512]{0,1:T(8,128)S(1)}, u32[]{:S(2)}, u32[]{:S(2)}) %collective-permute-start.2) | collective-permute-done | bytes 1048608 | tf_op jit(solution)/shard_map/ppermute | solution.py:12
  163.0 18.0 %collective-permute-done.3 = f32[512,512]{0,1:T(8,128)S(1)} collective-permute-done((f32[512,512]{0,1:T(8,128)S(1)}, f32[512,512]{0,1:T(8,128)S(1)}, u32[]{:S(2)}, u32[]{:S(2)}) %collective-permute-start.3) | collective-permute-done | bytes 1048608 | tf_op jit(solution)/shard_map/ppermute | solution.py:12
  181.2 8.8 %collective-permute-start.4 = (f32[512,512]{0,1:T(8,128)S(1)}, f32[512,512]{0,1:T(8,128)S(1)}, u32[]{:S(2)}, u32[]{:S(2)}) collective-permute-start(f32[512,512]{0,1:T(8,128)S(1)} %add.69), channel_id=1, source_target_pairs={{0,1},{1,0},{2,3},{3,2},{4,5},{5,4},{6,7},{7,6},{8,9},{9,8},{10,11... | collective-permute-start | bytes 3145736 | tf_op jit(solution)/shard_map/ppermute | solution.py:12
  190.0 2.3 collective-permute-done.4
  192.5 1.3 collective-permute-start.5
  193.8 23.2 %collective-permute-done.5 = f32[512,512]{0,1:T(8,128)S(1)} collective-permute-done((f32[512,512]{0,1:T(8,128)S(1)}, f32[512,512]{0,1:T(8,128)S(1)}, u32[]{:S(2)}, u32[]{:S(2)}) %collective-permute-start.5) | collective-permute-done | bytes 1048608 | tf_op jit(solution)/shard_map/ppermute | solution.py:12
  217.2 3.3 collective-permute-start.6
  220.5 22.2 %collective-permute-done.6 = f32[512,512]{0,1:T(8,128)S(1)} collective-permute-done((f32[512,512]{0,1:T(8,128)S(1)}, f32[512,512]{0,1:T(8,128)S(1)}, u32[]{:S(2)}, u32[]{:S(2)}) %collective-permute-start.6) | collective-permute-done | bytes 1048608 | tf_op jit(solution)/shard_map/ppermute | solution.py:12
  243.5 11.7 %cholesky.104 = f32[128,128]{1,0:T(8,128)S(1)} custom-call(f32[128,128]{1,0:T(8,128)S(1)} %cholesky.266), custom_call_target="Cholesky" | custom-call | tf_op jit(solution)/shard_map/jit(cholesky)/cholesky | solution.py:34
  255.3 9.8 %custom-call.31 = f32[1,128,128]{1,2,0:T(8,128)S(1)} custom-call(f32[1,128,128]{2,1,0:T(8,128)S(1)} %get-tuple-element.35), custom_call_target="InvertDiagBlocksLowerTriangular" | custom-call | tf_op jit(solution)/shard_map/jit(cholesky)/cholesky | solution.py:34
  265.9 11.7 %cholesky.217 = f32[128,128]{1,0:T(8,128)S(1)} custom-call(f32[128,128]{1,0:T(8,128)S(1)} %cholesky.270), custom_call_target="Cholesky" | custom-call | tf_op jit(solution)/shard_map/jit(cholesky)/cholesky | solution.py:34
  277.6 9.9 %custom-call.32 = f32[1,128,128]{1,2,0:T(8,128)S(1)} custom-call(f32[1,128,128]{2,1,0:T(8,128)S(1)} %get-tuple-element.32), custom_call_target="InvertDiagBlocksLowerTriangular" | custom-call | tf_op jit(solution)/shard_map/jit(cholesky)/cholesky | solution.py:34
  288.2 11.7 %cholesky.238 = f32[128,128]{1,0:T(8,128)S(1)} custom-call(f32[128,128]{1,0:T(8,128)S(1)} %cholesky.275), custom_call_target="Cholesky" | custom-call | tf_op jit(solution)/shard_map/jit(cholesky)/cholesky | solution.py:34
  300.7 9.8 %custom-call.33 = f32[1,128,128]{1,2,0:T(8,128)S(1)} custom-call(f32[1,128,128]{2,1,0:T(8,128)S(1)} %get-tuple-element.29), custom_call_target="InvertDiagBlocksLowerTriangular" | custom-call | tf_op jit(solution)/shard_map/jit(cholesky)/cholesky | solution.py:34
  311.1 11.7 %cholesky.255 = f32[128,128]{1,0:T(8,128)S(1)} custom-call(f32[128,128]{1,0:T(8,128)S(1)} %convolution_subtract_fusion.2), custom_call_target="Cholesky" | custom-call | tf_op jit(solution)/shard_map/jit(cholesky)/cholesky | solution.py:34
  327.2 8.0 %while.1 = (s32[]{:T(128)}, f32[512,512]{1,0:T(8,128)S(1)}, s32[4,2]{0,1:T(2,128)S(1)}, f32[4,128,128]{2,1,0:T(8,128)S(1)}, s32[]{:T(128)}) while((s32[]{:T(128)}, f32[512,512]{1,0:T(8,128)S(1)}, s32[4,2]{0,1:T(2,128)S(1)}, f32[4,128,128]{2,1,0:T(8,128)S(1)}, s32[]{:T(128)}) %tuple.33), condition=%wide.while_cond, body=%wide.while_body.sunk | while | flops 2 | bytes 131189 | solution.py:36
  327.8 1.4 bitcast_dynamic-update-slice_fusion.2
  329.8 1.4 bitcast_dynamic-update-slice_fusion.2
  331.8 1.4 bitcast_dynamic-update-slice_fusion.2
  333.8 1.4 bitcast_dynamic-update-slice_fusion.2
  335.2 39.3 %custom-call.34 = f32[4,128,128]{1,2,0:T(8,128)S(1)} custom-call(f32[4,128,128]{2,1,0:T(8,128)S(1)} %get-tuple-element.10), custom_call_target="InvertDiagBlocksLowerTriangular" | custom-call | tf_op jit(solution)/shard_map/jit(_solve_triangular)/triangular_solve | solution.py:36
  376.9 42.9 %all-gather.2.cloned.1.call-done = bf16[1024,512]{1,0:T(8,128)(2,1)} async-done(((bf16[64,512]{1,0:T(8,128)(2,1)}), bf16[1024,512]{1,0:T(8,128)(2,1)}) %all-gather.2.cloned.1.call-update) | async-done | bytes 1048592 | tf_op jit(solution)/shard_map/all_gather | solution.py:42
  419.8 11.5 %fusion.4 = f32[512,1,4096]{2,0,1:T(8,128)} fusion(bf16[1024,512]{1,0:T(8,128)(2,1)} %all-gather.2.cloned.1.call-done, bf16[1,1024,4096]{2,1,0:T(8,128)(2,1)} %param.2), kind=kOutput, calls=%fused_computation.6 | convolution fusion | flops 4294967296 | bytes 17825792 | tf_op jit(solution)/shard_map/nr,lnd->rld/dot_general | solution.py:40
  431.3 1.3 copy.8
  433.3 50.8 %reduce-scatter.5.cloned.1.call-done = f32[512,1,512]{2,0,1:T(8,128)} async-done(((f32[512,1,4096]{2,0,1:T(8,128)}), f32[512,1,512]{2,0,1:T(8,128)}) %reduce-scatter.5.cloned.1.call-update) | async-done | bytes 1048592 | tf_op jit(solution)/shard_map/reduce_scatter | solution.py:46
  484.1 1.3 broadcast_multiply_fusion
  485.4 2.0 copy.9
  (59 shorter events, 14.6 us)
Async XLA Ops:
  7.2 86.6 %reduce-scatter.3.cloned.1.call-start = ((), (), s32[]{:S(2)}) async-start(), calls=%async_computation.2 | async-start | bytes 2228224 | tf_op jit(solution)/shard_map/reduce_scatter | solution.py:24
  17.7 402.1 %all-gather.2.cloned.1.call-start = ((), (), s32[]{:S(2)}) async-start(), calls=%async_computation.3 | async-start | bytes 1114112 | tf_op jit(solution)/shard_map/all_gather | solution.py:42
  95.8 22.4 %collective-permute-start = (f32[512,512]{0,1:T(8,128)S(1)}, f32[512,512]{0,1:T(8,128)S(1)}, u32[]{:S(2)}, u32[]{:S(2)}) collective-permute-start(f32[512,512]{0,1:T(8,128)S(1)} %fusion.42), channel_id=1, source_target_pairs={{0,8},{8,0},{16,24},{24,16},{32,40},{40,32},{48,56},{56,48},{64,72... | collective-permute-start | bytes 3145736 | tf_op jit(solution)/shard_map/ppermute | solution.py:12
  118.4 23.0 %collective-permute-start.1 = (f32[512,512]{0,1:T(8,128)S(1)}, f32[512,512]{0,1:T(8,128)S(1)}, u32[]{:S(2)}, u32[]{:S(2)}) collective-permute-start(f32[512,512]{0,1:T(8,128)S(1)} %add.66), channel_id=1, source_target_pairs={{0,16},{8,24},{16,0},{24,8},{32,48},{40,56},{48,32},{56,40},{64,80... | collective-permute-start | bytes 3145736 | tf_op jit(solution)/shard_map/ppermute | solution.py:12
  141.7 20.6 %collective-permute-start.2 = (f32[512,512]{0,1:T(8,128)S(1)}, f32[512,512]{0,1:T(8,128)S(1)}, u32[]{:S(2)}, u32[]{:S(2)}) collective-permute-start(f32[512,512]{0,1:T(8,128)S(1)} %add.67), channel_id=1, source_target_pairs={{0,32},{8,40},{16,48},{24,56},{32,0},{40,8},{48,16},{56,24},{64,96... | collective-permute-start | bytes 3145736 | tf_op jit(solution)/shard_map/ppermute | solution.py:12
  162.5 18.5 %collective-permute-start.3 = (f32[512,512]{0,1:T(8,128)S(1)}, f32[512,512]{0,1:T(8,128)S(1)}, u32[]{:S(2)}, u32[]{:S(2)}) collective-permute-start(f32[512,512]{0,1:T(8,128)S(1)} %add.68), channel_id=1, source_target_pairs={{0,64},{8,72},{16,80},{24,88},{32,96},{40,104},{48,112},{56,120},{... | collective-permute-start | bytes 3145736 | tf_op jit(solution)/shard_map/ppermute | solution.py:12
  181.2 11.1 %collective-permute-start.4 = (f32[512,512]{0,1:T(8,128)S(1)}, f32[512,512]{0,1:T(8,128)S(1)}, u32[]{:S(2)}, u32[]{:S(2)}) collective-permute-start(f32[512,512]{0,1:T(8,128)S(1)} %add.69), channel_id=1, source_target_pairs={{0,1},{1,0},{2,3},{3,2},{4,5},{5,4},{6,7},{7,6},{8,9},{9,8},{10,11... | collective-permute-start | bytes 3145736 | tf_op jit(solution)/shard_map/ppermute | solution.py:12
  192.5 24.5 %collective-permute-start.5 = (f32[512,512]{0,1:T(8,128)S(1)}, f32[512,512]{0,1:T(8,128)S(1)}, u32[]{:S(2)}, u32[]{:S(2)}) collective-permute-start(f32[512,512]{0,1:T(8,128)S(1)} %add.70), channel_id=1, source_target_pairs={{0,2},{1,3},{2,0},{3,1},{4,6},{5,7},{6,4},{7,5},{8,10},{9,11},{10,... | collective-permute-start | bytes 3145736 | tf_op jit(solution)/shard_map/ppermute | solution.py:12
  217.2 25.5 %collective-permute-start.6 = (f32[512,512]{0,1:T(8,128)S(1)}, f32[512,512]{0,1:T(8,128)S(1)}, u32[]{:S(2)}, u32[]{:S(2)}) collective-permute-start(f32[512,512]{0,1:T(8,128)S(1)} %add.71), channel_id=1, source_target_pairs={{0,4},{1,5},{2,6},{3,7},{4,0},{5,1},{6,2},{7,3},{8,12},{9,13},{10,... | collective-permute-start | bytes 3145736 | tf_op jit(solution)/shard_map/ppermute | solution.py:12
  220.5 154.0 %copy-start = (f32[64,512]{1,0:T(8,128)S(1)}, f32[64,512]{1,0:T(8,128)}, u32[]{:S(2)}) copy-start(f32[64,512]{1,0:T(8,128)} %reduce-scatter.3.cloned.1.call-done) | copy-start | bytes 393220
  376.9 107.2 %reduce-scatter.5.cloned.1.call-start = ((), (), s32[]{:S(2)}) async-start(), calls=%async_computation.4 | async-start | bytes 9437184 | tf_op jit(solution)/shard_map/reduce_scatter | solution.py:46
Sparse Core Ops, SparseCore 0:
  17.8 75.9 reduce-scatter.2
  377.0 42.7 all-gather.1
  431.4 52.5 reduce-scatter.4
where the time goes:
time: 500 us; the launch traced here: 494 us
  waiting for transfers between devices  300 us (60%)
  other arithmetic  123 us (25%)
  matrix products  27.4 us (5%)
  between operations  16.8 us (3%)
  starting transfers between devices  16 us (3%)
  local copies, waits for them, and re-layouts  11.8 us (2%)
    ppermute x7, waiting for transfers between devices, swapped(): return lax.ppermute(value, axis, pairs)  130 us
    another operation x14, other arithmetic, on_device(): cholesky_factor = jnp.linalg.cholesky(gram_matrix)  78.7 us
    reduce_scatter x1, waiting for transfers between devices, on_device(): sample = lax.psum_scatter(summed, 'layer', scatter_dimension=0, tiled=True)  76.1 us
    reduce_scatter x1, waiting for transfers between devices, on_device(): lax.psum_scatter(partial_value, 'tok', scatter_dimension=2, tiled=True)  50.8 us
    all_gather x1, waiting for transfers between devices, on_device(): lax.all_gather(narrow, 'layer', axis=0, tiled=True)  42.9 us
    another operation x2, other arithmetic, on_device(): jax.scipy.linalg.solve_triangular(cholesky_factor, sample.T, lower=True)  39.3 us
    ppermute x7, starting transfers between devices, swapped(): return lax.ppermute(value, axis, pairs)  15.9 us
    dot_general x1, matrix products, on_device(): jnp.einsum('nr,lnd->rld', lax.all_gather(narrow, 'layer', axis=0, tiled=T...  11.5 us
  transfers between devices with their start and end apart: 10, of which 10 were waited for; matrix products, arithmetic and copies ran while one was open for 0% of the time, Pallas kernels for 0%

commit v1 on v0

v1 whole, which is shorter than its diff:
```python
import math

import jax
import jax.numpy as jnp
from jax import lax
from jax.experimental import pallas as pl
from jax.experimental.pallas import tpu as pltpu
from jax.sharding import PartitionSpec as P

HIGHEST = lax.Precision.HIGHEST
MESH = pl.DeviceIdType.MESH
F32 = jnp.float32
BF16 = jnp.bfloat16
SIDE = 4
HALF = 256


def dot_exact(a, b, ca, cb):
    dims = (((ca,), (cb,)), ((), ()))
    return lax.dot_general(a, b, dims, precision=HIGHEST, preferred_element_type=F32)


def row_of(value, index):
    return jnp.broadcast_to(value[index : index + 1, :], value.shape)


def col_of(value, index):
    return jnp.broadcast_to(value[:, index : index + 1], value.shape)


def eliminate(block):
    size = block.shape[0]
    count = size // 8
    rows = [block[8 * i : 8 * i + 8, :] for i in range(count)]
    sub = lax.broadcasted_iota(jnp.int32, (8, size), 0)
    lane = lax.broadcasted_iota(jnp.int32, (8, size), 1)
    reduced, pivots = [], []
    for b in range(count):
        x = rows[b]
        cols = [col_of(x, 8 * b + k) for k in range(8)]
        u = jnp.zeros_like(x)
        recips = jnp.zeros_like(x)
        pivot_rows = jnp.zeros_like(x)
        for s in range(8):
            at = lane == 8 * b + s
            here = sub == s
            pivot = row_of(cols[s], s)
            recip = 1.0 / pivot
            others = jnp.where(here, 0.0, cols[s])
            row = row_of(x, s)
            u = jnp.where(here, row, u)
            pivot_rows = jnp.where(here, pivot, pivot_rows)
            recips = jnp.where(here, recip, recips)
            row = jnp.where(at, 1.0, row)
            x = jnp.where(at, jnp.where(here, 1.0, 0.0), x) - (others * row) * recip
            for k in range(s + 1, 8):
                cols[k] = cols[k] - (others * row_of(cols[k], s)) * recip
        reduced.append(u)
        pivots.append(pivot_rows)
        if b + 1 < count:
            solved = x * recips
            solved_rows = [row_of(solved, k) for k in range(8)]
            inside = (lane >= 8 * b) & (lane < 8 * b + 8)
            for i in range(b + 1, count):
                y = rows[i]
                t = [col_of(y, 8 * b + k) * solved_rows[k] for k in range(8)]
                t = ((t[0] + t[1]) + (t[2] + t[3])) + ((t[4] + t[5]) + (t[6] + t[7]))
                rows[i] = jnp.where(inside, 0.0, y) - t
    return jnp.concatenate(reduced, 0), jnp.concatenate(pivots, 0)


def factor_block(block):
    reduced, pivots = eliminate(block)
    row = lax.broadcasted_iota(jnp.int32, reduced.shape, 0)
    lane = lax.broadcasted_iota(jnp.int32, reduced.shape, 1)
    scale = lax.rsqrt(pivots)
    upper = jnp.where(lane >= row, reduced, 0.0) * scale
    inverse = jnp.where(lane < row, reduced, jnp.where(lane == row, 1.0, 0.0)) * scale
    return upper, inverse


def cholesky_panel(gram, upper, inverse, start, width):
    size = gram.shape[0]
    stop = start + width
    own = slice(start, stop)
    r, w = factor_block(gram[own, own])
    upper[own, own] = r
    inverse[own, own] = w
    if stop < size:
        rest = slice(stop, size)
        r_rest = dot_exact(w, gram[own, rest], 1, 0)
        upper[own, rest] = r_rest
        upper[rest, own] = jnp.zeros((size - stop, width), F32)
        inverse[own, rest] = jnp.zeros((width, size - stop), F32)
        gram[rest, rest] = gram[rest, rest] - dot_exact(r_rest, r_rest, 0, 0)
    if start:
        before = slice(0, start)
        t = dot_exact(upper[before, own], inverse[before, before], 0, 0)
        inverse[own, before] = -dot_exact(w, t, 1, 0)


def kernel(
    a_hbm, k_hbm,
    q_out, r_out, d_out,
    a, k, part, rx1, rx2, rz1, rz2, px, pz, sg, hi, lo,
    gb, gc, gy, gram, inv,
    away, home, pair, fwd, near,
    load_sem, send_sem, recv_sem,
):
    layer, tok = lax.axis_index("layer"), lax.axis_index("tok")
    z, x = lax.div(layer, SIDE), lax.rem(layer, SIDE)
    y, c = lax.div(tok, 2), lax.rem(tok, 2)
    total_rows = 8 * part.shape[0] * part.shape[1] * part.shape[2]

    def plus(value, step):
        return lax.rem(value + (step + SIDE), SIDE)

    def at_z(step):
        return (plus(z, step) * SIDE + x, tok)

    def at_x(step):
        return (z * SIDE + plus(x, step), tok)

    def at_y(step):
        return (layer, plus(y, step) * 2 + c)

    other_core = (layer, y * 2 + (1 - c))

    used = [0]
    sent, gram_sent = [], []

    def slots(count):
        first = used[0]
        used[0] += count
        return first

    def copy(src, dst, slot, device):
        return pltpu.make_async_remote_copy(
            src_ref=src, dst_ref=dst, send_sem=send_sem.at[slot], recv_sem=recv_sem.at[slot],
            device_id=device, device_id_type=MESH,
        )

    def put(src, dst, slot, device, log=sent):
        sending = copy(src, dst, slot, device)
        sending.start()
        log.append(sending)

    def take(dst, slot, device):
        copy(dst, dst, slot, device).wait_recv()

    barrier = pltpu.get_barrier_semaphore()
    friends = [at_z(s) for s in (1, 2, 3)] + [at_x(s) for s in (1, 2, 3)] + [at_y(s) for s in (1, 2, 3)] + [other_core]
    for friend in friends:
        pl.semaphore_signal(barrier, inc=1, device_id=friend, device_id_type=MESH)

    rows = a.shape[0] // SIDE
    k_load = pltpu.make_async_copy(k_hbm.at[0], k, load_sem.at[SIDE])
    k_load.start()
    chunk_z = [plus(z, i) for i in (1, 2, 3, 0)]
    loads = []
    for i, cz in enumerate(chunk_z):
        span = pl.ds(pl.multiple_of(cz * rows, rows), rows)
        loads.append(pltpu.make_async_copy(a_hbm.at[0, span, :], a.at[span, :], load_sem.at[i]))
        loads[-1].start()
    k_load.wait()

    low, high = pl.ds(0, HALF), pl.ds(HALF, HALF)
    x1, z1, x2, z2 = slots(12), slots(3), slots(3), slots(3)
    for i, cz in enumerate(chunk_z):
        loads[i].wait()
        span = pl.ds(pl.multiple_of(cz * rows, rows), rows)

        @pl.loop(0, 2)
        def _(h):
            cols = pl.ds(pl.multiple_of(h * HALF, HALF), HALF)
            terms = jnp.dot(a[span, :], k[:, cols], preferred_element_type=F32)
            part[cz, :, :, cols] = terms.reshape(part.shape[1], part.shape[2], HALF)

        if i == 0:
            pl.semaphore_wait(barrier, len(friends))
        for s in (1, 2, 3):
            put(part.at[cz, plus(x, s), :, low], rx1.at[s - 1, cz], x1 + 4 * (s - 1) + i, at_x(s))
        if i < 3:
            put(part.at[cz, :, :, high], rz1.at[i], z1 + i, at_z(i + 1))

    for i, cz in enumerate(chunk_z):
        for s in (1, 2, 3):
            take(rx1.at[s - 1, cz], x1 + 4 * (s - 1) + i, at_x(-s))
        px[cz] = (part[cz, x, :, low] + rx1[0, cz]) + (rx1[1, cz] + rx1[2, cz])
        if i < 3:
            put(px.at[cz], rx2.at[i], x2 + i, at_z(i + 1))
    for s in (1, 2, 3):
        take(rz1.at[s - 1], z1 + s - 1, at_z(-s))
    pz[...] = (part[z, :, :, high] + rz1[0]) + (rz1[1] + rz1[2])
    for s in (1, 2, 3):
        put(pz.at[plus(x, s)], rz2.at[s - 1], z2 + s - 1, at_x(s))
    for s in (1, 2, 3):
        take(rx2.at[s - 1], x2 + s - 1, at_z(-s))
    sg[z, x, :, low] = (px[z] + rx2[0]) + (rx2[1] + rx2[2])

    xa, xb, za, zb = slots(3), slots(12), slots(3), slots(12)
    for s in (1, 2, 3):
        put(sg.at[z, x, :, low], sg.at[z, x, :, low], xa + s - 1, at_z(s))
    for s in (1, 2, 3):
        put(sg.at[z, x, :, low], sg.at[z, x, :, low], xb + s - 1, at_x(s))
    for s in (1, 2, 3):
        take(rz2.at[s - 1], z2 + s - 1, at_x(-s))
    sg[z, x, :, high] = (pz[x] + rz2[0]) + (rz2[1] + rz2[2])
    for s in (1, 2, 3):
        put(sg.at[z, x, :, high], sg.at[z, x, :, high], za + s - 1, at_x(s))
    for s in (1, 2, 3):
        put(sg.at[z, x, :, high], sg.at[z, x, :, high], zb + s - 1, at_z(s))
    for m in (1, 2, 3):
        mz, mx = plus(z, -m), plus(x, -m)
        take(sg.at[mz, x, :, low], xa + m - 1, at_z(-m))
        for s in (1, 2, 3):
            put(sg.at[mz, x, :, low], sg.at[mz, x, :, low], xb + 3 * m + s - 1, at_x(s))
        take(sg.at[z, mx, :, high], za + m - 1, at_x(-m))
        for s in (1, 2, 3):
            put(sg.at[z, mx, :, high], sg.at[z, mx, :, high], zb + 3 * m + s - 1, at_z(s))
    for m in range(4):
        mz, mx = plus(z, -m), plus(x, -m)
        for s in (1, 2, 3):
            take(sg.at[mz, plus(x, -s), :, low], xb + 3 * m + s - 1, at_x(-s))
            take(sg.at[plus(z, -s), mx, :, high], zb + 3 * m + s - 1, at_z(-s))

    wide = 128
    block_rows = pl.ds(pl.multiple_of(z * wide, wide), wide)
    block_cols = pl.ds(pl.multiple_of(x * wide, wide), wide)
    group = part.shape[0] * part.shape[1] * part.shape[2]
    left = sg[:, :, :, block_rows].reshape(group, wide)
    right = sg[:, :, :, block_cols].reshape(group, wide)
    gb[...] = dot_exact(left, right, 0, 0).reshape(2, wide // 2, wide) * (1.0 / total_rows)
    g_core = slots(1)
    put(gb.at[1 - c], gc, g_core, other_core)

    @pl.loop(0, SIDE)
    def _(i):
        value = sg[i].reshape(group // SIDE, sg.shape[3]).T
        top = value.astype(BF16)
        cols = pl.ds(pl.multiple_of(i * (group // SIDE), group // SIDE), group // SIDE)
        hi[:, cols] = top
        lo[:, cols] = (value - top.astype(F32)).astype(BF16)

    width = d_out.shape[1]

    def project(dst, step, core):
        owner = plus(y, step) * 2 + core

        @pl.loop(0, width // HALF)
        def _(h):
            cols = pl.ds(pl.multiple_of(owner * width + h * HALF, HALF), HALF)
            block = a[:, cols]
            value = jnp.dot(hi[...], block, preferred_element_type=F32)
            value = value + jnp.dot(lo[...], block, preferred_element_type=F32)
            dst[:, pl.ds(pl.multiple_of(h * HALF, HALF), HALF)] = value

    p_core = slots(4)
    order = (2, 1, 3, 0)

    def project_both(i):
        project(away.at[i], order[i], 1 - c)
        put(away.at[i], pair.at[i], p_core + i, other_core)
        project(home.at[i], order[i], c)

    def add_pair(i):
        take(pair.at[i], p_core + i, other_core)
        home[i] = home[i] + pair[i]

    top, bottom = pl.ds(0, HALF), pl.ds(HALF, HALF)
    f_up, f_down, n_up, n_down = slots(1), slots(1), slots(2), slots(2)
    g_y, ga, gbx, gaz, gbz, g_swap = slots(3), slots(3), slots(12), slots(3), slots(12), slots(1)

    project_both(0)
    take(gc, g_core, other_core)
    gy[y] = gb[c] + gc[...]
    for s in (1, 2, 3):
        put(gy.at[y], gy.at[y], g_y + s - 1, at_y(s))
    project_both(1)
    add_pair(0)
    put(home.at[0, top, :], fwd.at[0], f_up, at_y(1))
    put(home.at[0, bottom, :], fwd.at[1], f_down, at_y(-1))

    def piece(pz_, px_, part_index):
        r = pl.ds(pl.multiple_of(pz_ * wide + c * (wide // 2) + part_index * (wide // 4), wide // 4), wide // 4)
        return gram.at[r, pl.ds(pl.multiple_of(px_ * wide, wide), wide)]

    for s in (1, 2, 3):
        take(gy.at[plus(y, -s)], g_y + s - 1, at_y(-s))
    mine = pl.ds(pl.multiple_of(z * wide + c * (wide // 2), wide // 2), wide // 2)
    gram[mine, block_cols] = (gy[0] + gy[1]) + (gy[2] + gy[3])
    for s in (1, 2, 3):
        put(piece(z, x, 0), piece(z, x, 0), ga + s - 1, at_z(s), gram_sent)
        put(piece(z, x, 1), piece(z, x, 1), gaz + s - 1, at_x(s), gram_sent)
    for s in (1, 2, 3):
        put(piece(z, x, 0), piece(z, x, 0), gbx + s - 1, at_x(s), gram_sent)
        put(piece(z, x, 1), piece(z, x, 1), gbz + s - 1, at_z(s), gram_sent)
    project_both(2)
    for m in (1, 2, 3):
        mz, mx = plus(z, -m), plus(x, -m)
        take(piece(mz, x, 0), ga + m - 1, at_z(-m))
        for s in (1, 2, 3):
            put(piece(mz, x, 0), piece(mz, x, 0), gbx + 3 * m + s - 1, at_x(s), gram_sent)
        take(piece(z, mx, 1), gaz + m - 1, at_x(-m))
        for s in (1, 2, 3):
            put(piece(z, mx, 1), piece(z, mx, 1), gbz + 3 * m + s - 1, at_z(s), gram_sent)
    add_pair(1)
    put(home.at[1, bottom, :], near.at[0, bottom, :], n_up, at_y(1))
    project_both(3)
    for m in range(4):
        mz, mx = plus(z, -m), plus(x, -m)
        for s in (1, 2, 3):
            take(piece(mz, plus(x, -s), 0), gbx + 3 * m + s - 1, at_x(-s))
            take(piece(plus(z, -s), mx, 1), gbz + 3 * m + s - 1, at_z(-s))
    for i in range(SIDE):
        rows_here = pl.ds(pl.multiple_of(i * wide + c * (wide // 2), wide // 2), wide // 2)
        if i == 0:
            g_swaps = slots(SIDE)
        put(gram.at[rows_here, :], gram.at[rows_here, :], g_swaps + i, other_core, gram_sent)
    add_pair(2)
    put(home.at[2, top, :], near.at[1, top, :], n_down, at_y(-1))
    add_pair(3)
    for i in range(SIDE):
        rows_there = pl.ds(pl.multiple_of(i * wide + (1 - c) * (wide // 2), wide // 2), wide // 2)
        take(gram.at[rows_there, :], g_swaps + i, other_core)

    for sending in gram_sent:
        sending.wait_send()
    cholesky_panel(gram, r_out, inv, 0, wide)
    take(fwd.at[0], f_up, at_y(-1))
    home[1, top, :] = home[1, top, :] + fwd[0]
    put(home.at[1, top, :], near.at[0, top, :], n_up + 1, at_y(1))
    take(fwd.at[1], f_down, at_y(1))
    home[2, bottom, :] = home[2, bottom, :] + fwd[1]
    put(home.at[2, bottom, :], near.at[1, bottom, :], n_down + 1, at_y(-1))
    for start in range(wide, gram.shape[0], wide):
        cholesky_panel(gram, r_out, inv, start, wide)

    own = sg[z, x]
    q_out[...] = dot_exact(own, inv[...], 1, 1)
    take(near.at[0, bottom, :], n_up, at_y(-1))
    take(near.at[1, top, :], n_down, at_y(1))
    take(near.at[0, top, :], n_up + 1, at_y(-1))
    take(near.at[1, bottom, :], n_down + 1, at_y(1))
    scale = 1.0 / math.sqrt(total_rows)

    @pl.loop(0, width // HALF)
    def _(h):
        cols = pl.ds(pl.multiple_of(h * HALF, HALF), HALF)
        total = (home[3, :, cols] + near[0, :, cols]) + near[1, :, cols]
        d_out[:, cols] = dot_exact(inv[...], total * scale, 1, 0)

    for sending in sent:
        sending.wait_send()


def on_device(activations, sketch):
    _, rows, depth = activations.shape
    rank = sketch.shape[2]
    strip = rows // 16
    width = depth // 8
    vmem = pltpu.VMEM
    q, r, d = pl.pallas_call(
        kernel,
        out_shape=(
            jax.ShapeDtypeStruct((strip, rank), F32),
            jax.ShapeDtypeStruct((rank, rank), F32),
            jax.ShapeDtypeStruct((rank, width), F32),
        ),
        in_specs=[pl.BlockSpec(memory_space=pl.ANY)] * 2,
        out_specs=(pl.BlockSpec(memory_space=pltpu.VMEM),) * 3,
        scratch_shapes=[
            vmem((rows, depth), BF16),
            vmem((depth, rank), BF16),
            vmem((4, 4, strip, rank), F32),
            vmem((3, 4, strip, HALF), F32),
            vmem((3, strip, HALF), F32),
            vmem((3, 4, strip, HALF), F32),
            vmem((3, strip, HALF), F32),
            vmem((4, strip, HALF), F32),
            vmem((4, strip, HALF), F32),
            vmem((4, 4, strip, rank), F32),
            vmem((rank, rows), BF16),
            vmem((rank, rows), BF16),
            vmem((2, 64, 128), F32),
            vmem((64, 128), F32),
            vmem((4, 64, 128), F32),
            vmem((rank, rank), F32),
            vmem((rank, rank), F32),
            vmem((4, rank, width), F32),
            vmem((4, rank, width), F32),
            vmem((4, rank, width), F32),
            vmem((2, HALF, width), F32),
            vmem((2, rank, width), F32),
            pltpu.SemaphoreType.DMA((5,)),
            pltpu.SemaphoreType.DMA((112,)),
            pltpu.SemaphoreType.DMA((112,)),
        ],
        compiler_params=pltpu.CompilerParams(
            collective_id=0, has_side_effects=True, vmem_limit_bytes=56 << 20
        ),
        cost_estimate=pl.CostEstimate(flops=16 * rows * depth * rank, bytes_accessed=16 << 20, transcendentals=0),
    )(activations, sketch)
    return q.reshape(1, 1, strip, rank), r, d.reshape(rank, 1, width)


def solution(mesh):
    return jax.shard_map(
        on_device,
        mesh=mesh,
        in_specs=(P("layer", "tok", None), P("layer", None, None)),
        out_specs=(P("tok", "layer", None, None), P(), P(None, "layer", "tok")),
        check_vma=False,
    )
```

time: 500 us -> 101 us (0.20); the launches traced: 494 us -> 101 us
  waiting for transfers between devices: 300 us -> 0 us
  other arithmetic: 123 us -> 0 us
  Pallas kernels: 0 us -> 93.3 us
  matrix products: 27.4 us -> 0 us
  between operations: 16.8 us -> 0.64 us
  starting transfers between devices: 16 us -> 0 us
    ppermute x7 -> x0, waiting for transfers between devices: 130 us -> none  [swapped(): return lax.ppermute(value, axis, pairs)]
    reduce_scatter x2 -> x0, waiting for transfers between devices: 127 us -> none  [the longest x1 76.1 us: on_device(): sample = lax.psum_scatter(summed, 'layer', scatter_dimension=0, tiled=True)]
    another operation x16 -> x0, other arithmetic: 118 us -> none  [the longest x14 78.7 us: on_device(): cholesky_factor = jnp.linalg.cholesky(gram_matrix)]
    pallas_call x0 -> x1, Pallas kernels: none -> 93.3 us  [on_device(): pl.pallas_call(kernel, out_shape=(jax.ShapeDtypeStruct((strip, rank), F32...]
    all_gather x1 -> x0, waiting for transfers between devices: 42.9 us -> none  [on_device(): lax.all_gather(narrow, 'layer', axis=0, tiled=True)]
    dot_general x3 -> x0, matrix products: 23.9 us -> none  [the longest x1 11.5 us: on_device(): jnp.einsum('nr,lnd->rld', lax.all_gather(narrow, 'layer', axis=0, tiled=T...]
    ppermute x7 -> x0, starting transfers between devices: 15.9 us -> none  [swapped(): return lax.ppermute(value, axis, pairs)]
    another operation x17 -> x0, local copies, waits for them, and re-layouts: 8.06 us -> none
  transfers between devices with their start and end apart: 10 -> 0, of which waited for: 10 -> 0; matrix products, arithmetic and copies ran while one was open for 0% -> 0% of each run, Pallas kernels for 0% -> 0%
where the time goes in v1:
time: 101 us
  Pallas kernels  93.3 us (92%)
  local copies, waits for them, and re-layouts  7.1 us (7%)
    pallas_call x1, Pallas kernels, on_device(): pl.pallas_call(kernel, out_shape=(jax.ShapeDtypeStruct((strip, rank), F32...  93.3 us
    unnamed x3, local copies, waits for them, and re-layouts  7.1 us

profile of v1, /device:TPU:1, one launch (start us, length us, event | category | flops | bytes accessed | tf_op | source)
XLA Modules:
  0.0 101.1 jit_solution(7413050562430910294)
XLA Ops:
  0.6 93.3 %shard_map.49 = (f32[64,512]{1,0:T(8,128)}, f32[512,512]{1,0:T(8,128)}, f32[512,512]{1,0:T(8,128)}) custom-call(bf16[1,1024,4096]{2,1,0:T(8,128)(2,1)} %a_hbm.1, bf16[1,4096,512]{2,1,0:T(8,128)(2,1)} %k_hbm.1), custom_call_target="tpu_custom_call" | custom-call | flops 34359738368 | bytes 16777216 | tf_op jit(solution)/shard_map/pallas_call | solution.py:363
  94.0 3.3 %copy.5 = f32[512,1,512]{2,1,0:T(1,128)} copy(f32[512,1,512]{2,0,1:T(8,128)} %bitcast.2) | data formatting | bytes 2097152
  97.2 1.6 %copy.8 = f32[1,1,64,512]{3,2,1,0:T(8,128)} copy(f32[1,1,64,512]{3,2,1,0:T(8,128)} %bitcast.3) | data formatting | bytes 262144
  98.8 2.3 %copy.9 = f32[512,512]{1,0:T(8,128)} copy(f32[512,512]{1,0:T(8,128)} %get-tuple-element.16) | data formatting | bytes 2097152
